TPU v7x, 512 devices: a whole 4x8x8 slice. The times are simulated.
512 devices in a mesh: pipe: 16 (over z, x_lo), expert: 32 (over y, x_hi, core).
Axes of the slice: x: 4 (x_hi: 2, x_lo: 2; x = x_hi * 2 + x_lo), y: 8, z: 8, core: 2. Of those that a mesh axis runs over, the one named last changes fastest.
Arguments:
- fwd_tokens: bfloat16 [16, 2048, 3584], P('pipe', 'expert'), may hold values from -6 to 6
- bwd_tokens: bfloat16 [16, 2048, 3584], P('pipe', 'expert'), may hold values from -6 to 6
- bwd_cotangent: bfloat16 [16, 2048, 3584], P('pipe', 'expert'), may hold values from -6 to 6
- fwd_routes: int32 [16, 2048, 8], P('pipe', 'expert'), may hold values from 0 to 255, as said below
- bwd_routes: int32 [16, 2048, 8], P('pipe', 'expert'), may hold values from 0 to 255, as said below
- router_weight: bfloat16 [16, 3584, 256], P('pipe', 'expert'), may hold values from -0.09375 to 0.09375
- up_weight: bfloat16 [16, 3584, 4096], P('pipe', None, 'expert'), may hold values from -0.09375 to 0.09375
- down_weight: bfloat16 [16, 4096, 3584], P('pipe', 'expert'), may hold values from -0.1875 to 0.1875
Outputs:
- fwd_next: bfloat16 [16, 2048, 3584], P('pipe', 'expert')
- bwd_next: bfloat16 [16, 2048, 3584], P('pipe', 'expert')
Inputs may be any that keep to these rules, and one draw needn't show every extreme that they name: `fwd_routes`: each row names 8 different experts. For each expert below 4, the 64 rows of one device name it at most 8 times; in every section some expert below 4 is named exactly 8 times by the rows of every device. `bwd_routes`: as for fwd_routes.
All inputs are finite; a program needn't handle non-finite values.
Results may differ from a plain program's by a relative error of at most 0.015.
Values may be sent and summed in bfloat16 or wider, within the bound.
A program may use at most 64 MiB of HBM per device.

v0:
```python
import jax
import jax.numpy as jnp
from jax import lax
from jax.sharding import PartitionSpec as P

SLICES = 8
CAP = 8


route_scale = 2.5
highest = lax.Precision.HIGHEST


def passed_along(block, axis, distance):
    devices = range(lax.axis_size(axis))
    route = [((i - distance) % len(devices), i) for i in devices]
    return lax.ppermute(block, axis, route)


def silu_slope(values):
    logistic = jax.nn.sigmoid(values)
    return logistic * (1.0 + values * (1.0 - logistic))


def routed_gates(token_rows, routes, router_weight):
    logits = jnp.dot(token_rows, router_weight, preferred_element_type=jnp.float32)
    scores = jax.nn.sigmoid(logits)
    expert_ids = lax.broadcasted_iota(jnp.int32, (1, 1, router_weight.shape[1]), 2)
    picks = (routes[:, :, None] == expert_ids).astype(jnp.float32)
    chosen = jnp.einsum("tke,te->tk", picks, scores, precision=highest)
    score_sum = jnp.sum(chosen, axis=1, keepdims=True)
    return (scores, picks, chosen, score_sum, route_scale * chosen / score_sum)


def slot_layout(routes, gates, flight):
    flight_hits = (routes[:, :, None] == lax.broadcasted_iota(jnp.int32, (1, 1, flight), 2)).astype(
        jnp.float32
    )
    member = jnp.sum(flight_hits, axis=1)
    flight_gate = jnp.einsum("tkf,tk->tf", flight_hits, gates, precision=highest)
    placing = jnp.cumsum(member, axis=0) - 1.0
    slot_ids = lax.broadcasted_iota(jnp.float32, (1, CAP, 1), 1)
    select = member.T[:, None, :] * (placing.T[:, None, :] == slot_ids).astype(jnp.float32)
    return (flight_hits, select, flight_gate)


def pack_rows(select, token_rows):
    packed = jnp.einsum(
        "fct,td->fcd", select.astype(jnp.bfloat16), token_rows, preferred_element_type=jnp.float32
    ).astype(jnp.bfloat16)
    flight_count, slot_count, model_width = packed.shape
    outgoing = jnp.broadcast_to(packed[:, None], (flight_count, SLICES, slot_count, model_width))
    return (packed, outgoing.reshape(flight_count * SLICES, slot_count, model_width))


def slice_sum(returned, flight):
    return jnp.sum(
        returned.reshape((flight, SLICES) + returned.shape[1:]).astype(jnp.float32), axis=1
    )


def spread(select, flight_gate, values):
    weights = select * flight_gate.T[:, None, :]
    return jnp.einsum("fct,fcd->td", weights, values, precision=highest)


def on_device(
    fwd_tokens,
    bwd_tokens,
    bwd_cotangent,
    fwd_routes,
    bwd_routes,
    router_weight,
    up_weight,
    down_weight,
):
    router_local = lax.all_gather(router_weight[0], "expert", axis=0, tiled=True)
    up_local = up_weight[0]
    down_local = down_weight[0]
    flight = lax.axis_size("expert") // SLICES
    _, _, _, _, gates_fwd = routed_gates(fwd_tokens[0], fwd_routes[0], router_local)
    _, select_fwd, flight_gate_fwd = slot_layout(fwd_routes[0], gates_fwd, flight)
    _, outgoing_fwd = pack_rows(select_fwd, fwd_tokens[0])
    pre_act = jnp.einsum(
        "scd,dh->sch",
        lax.all_to_all(outgoing_fwd, "expert", split_axis=0, concat_axis=0, tiled=True),
        up_local,
        preferred_element_type=jnp.float32,
    )
    activation = jax.nn.silu(pre_act).astype(jnp.bfloat16)
    shares_fwd = jnp.einsum(
        "sch,hd->scd", activation, down_local, preferred_element_type=jnp.float32
    ).astype(jnp.bfloat16)
    returned_fwd = lax.all_to_all(shares_fwd, "expert", split_axis=0, concat_axis=0, tiled=True)
    layer_fwd = spread(select_fwd, flight_gate_fwd, slice_sum(returned_fwd, flight)).astype(
        jnp.bfloat16
    )
    fwd_next = passed_along(layer_fwd, "pipe", 1)
    scores_bwd, picks_bwd, chosen_bwd, score_sum, gates_bwd = routed_gates(
        bwd_tokens[0], bwd_routes[0], router_local
    )
    hits_bwd, select_bwd, flight_gate_bwd = slot_layout(bwd_routes[0], gates_bwd, flight)
    _, outgoing_bwd = pack_rows(select_bwd, bwd_tokens[0])
    packed_cot, outgoing_cot = pack_rows(select_bwd, bwd_cotangent[0])
    received = lax.all_to_all(outgoing_bwd, "expert", split_axis=0, concat_axis=0, tiled=True)
    incoming = lax.all_to_all(outgoing_cot, "expert", split_axis=0, concat_axis=0, tiled=True)
    pre_act = jnp.einsum("scd,dh->sch", received, up_local, preferred_element_type=jnp.float32)
    activation = jax.nn.silu(pre_act).astype(jnp.bfloat16)
    part_rows = jnp.einsum(
        "sch,hd->scd", activation, down_local, preferred_element_type=jnp.float32
    ).astype(jnp.bfloat16)
    act_grad = jnp.einsum("scd,hd->sch", incoming, down_local, preferred_element_type=jnp.float32)
    pre_grad = (act_grad * silu_slope(pre_act)).astype(jnp.bfloat16)
    grad_rows = jnp.einsum(
        "sch,dh->scd", pre_grad, up_local, preferred_element_type=jnp.float32
    ).astype(jnp.bfloat16)
    grad_back, parts_back = (
        lax.all_to_all(grad_rows, "expert", split_axis=0, concat_axis=0, tiled=True),
        lax.all_to_all(part_rows, "expert", split_axis=0, concat_axis=0, tiled=True),
    )
    split_parts = parts_back.reshape((flight, SLICES) + parts_back.shape[1:])
    slice_dots = jnp.einsum(
        "fcd,fscd->fsc", packed_cot, split_parts, preferred_element_type=jnp.float32
    ).astype(jnp.bfloat16)
    flight_dots = jnp.sum(slice_dots.astype(jnp.float32), axis=1)
    token_dots = jnp.einsum("fc,fct->tf", flight_dots, select_bwd, precision=highest)
    gate_grad = jnp.einsum("tkf,tf->tk", hits_bwd, token_dots, precision=highest)
    weighted = jnp.sum(gate_grad * chosen_bwd, axis=1, keepdims=True) / score_sum
    pick_grad = route_scale / score_sum * (gate_grad - weighted)
    score_grad = jnp.einsum("tke,tk->te", picks_bwd, pick_grad, precision=highest)
    logit_grad = (score_grad * scores_bwd * (1.0 - scores_bwd)).astype(jnp.bfloat16)
    router_term = lax.dot_general(
        logit_grad, router_local, (((1,), (1,)), ((), ())), preferred_element_type=jnp.float32
    )
    expert_term = spread(select_bwd, flight_gate_bwd, slice_sum(grad_back, flight))
    layer_bwd = (expert_term + router_term).astype(jnp.bfloat16)
    bwd_next = passed_along(layer_bwd, "pipe", 1)
    return (fwd_next[None], bwd_next[None])


def solution(mesh):
    in_specs = (
        P("pipe", "expert", None),
        P("pipe", "expert", None),
        P("pipe", "expert", None),
        P("pipe", "expert", None),
        P("pipe", "expert", None),
        P("pipe", "expert", None),
        P("pipe", None, "expert"),
        P("pipe", "expert", None),
    )
    out_specs = (P("pipe", "expert", None), P("pipe", "expert", None))
    return jax.shard_map(
        on_device, mesh=mesh, in_specs=in_specs, out_specs=out_specs, check_vma=False
    )
```

profile of v0, /device:TPU:1, one launch (start us, length us, event | category | flops | bytes accessed | tf_op | source)
XLA Modules:
  0.0 366.9 jit_solution(4236724325431582800)
XLA Ops:
  7.2 0.8 convert_reduce_fusion.3
  8.2 1.2 convolution_convert_fusion.3
  9.5 1.4 broadcast_in_dim.13
  10.9 11.3 %all-to-all-start.3 = ((bf16[32,8,3584]{2,1,0:T(8,128)(2,1)}), bf16[32,8,3584]{2,1,0:T(8,128)(2,1)S(1)}, u32[]{:S(2)}, u32[]{:S(2)}) async-start(bf16[32,8,3584]{2,1,0:T(8,128)(2,1)} %bitcast.138), calls=%async_computation.3 | async-start | bytes 3670016 | tf_op jit(solution)/shard_map/all_to_all | solution.py:105
  22.4 44.4 %all-to-all-done.3 = bf16[32,8,3584]{2,1,0:T(8,128)(2,1)S(1)} async-done(((bf16[32,8,3584]{2,1,0:T(8,128)(2,1)}), bf16[32,8,3584]{2,1,0:T(8,128)(2,1)S(1)}, u32[]{:S(2)}, u32[]{:S(2)}) %all-to-all-start.3) | async-done | bytes 1835040 | tf_op jit(solution)/shard_map/all_to_all | solution.py:105
  66.8 1.5 broadcast_in_dim.12
  68.6 6.3 %all-to-all-start.2 = ((bf16[32,8,3584]{2,1,0:T(8,128)(2,1)}), bf16[32,8,3584]{2,1,0:T(8,128)(2,1)}, u32[]{:S(2)}, u32[]{:S(2)}) async-start(bf16[32,8,3584]{2,1,0:T(8,128)(2,1)} %bitcast.136), calls=%async_computation.2 | async-start | bytes 3670016 | tf_op jit(solution)/shard_map/all_to_all | solution.py:106
  75.7 2.1 fusion.42
  77.9 1.9 convolution_convert_fusion
  79.8 41.0 %all-to-all-done.2 = bf16[32,8,3584]{2,1,0:T(8,128)(2,1)} async-done(((bf16[32,8,3584]{2,1,0:T(8,128)(2,1)}), bf16[32,8,3584]{2,1,0:T(8,128)(2,1)}, u32[]{:S(2)}, u32[]{:S(2)}) %all-to-all-start.2) | async-done | bytes 1835040 | tf_op jit(solution)/shard_map/all_to_all | solution.py:106
  120.8 6.6 %all-to-all-start.5 = ((bf16[32,8,3584]{2,1,0:T(8,128)(2,1)}), bf16[32,8,3584]{2,1,0:T(8,128)(2,1)}, u32[]{:S(2)}, u32[]{:S(2)}) async-start(bf16[32,8,3584]{2,1,0:T(8,128)(2,1)} %convolution_convert_fusion), calls=%async_computation.5 | async-start | bytes 3670016 | tf_op jit(solution)/shard_map/all_to_all | solution.py:119
  127.5 49.4 %all-gather.3.cloned.1.call-done = bf16[1,3584,256]{2,1,0:T(8,128)(2,1)} async-done(((bf16[1,112,256]{2,1,0:T(8,128)(2,1)}), bf16[1,3584,256]{2,1,0:T(8,128)(2,1)}) %all-gather.3.cloned.1.call-update) | async-done | bytes 1835024 | tf_op jit(solution)/shard_map/all_gather | solution.py:77
  176.9 2.0 fusion.22
  180.6 1.4 broadcast_in_dim.10
  182.0 7.4 %all-to-all-start = ((bf16[32,8,3584]{2,1,0:T(8,128)(2,1)}), bf16[32,8,3584]{2,1,0:T(8,128)(2,1)}, u32[]{:S(2)}, u32[]{:S(2)}) async-start(bf16[32,8,3584]{2,1,0:T(8,128)(2,1)} %bitcast.137), calls=%async_computation | async-start | bytes 3670016 | tf_op jit(solution)/shard_map/all_to_all | solution.py:86
  189.3 4.8 %convolution_convert_fusion.1 = bf16[32,8,3584]{2,1,0:T(8,128)(2,1)} fusion(bf16[32,8,3584]{2,1,0:T(8,128)(2,1)} %all-to-all-done.2, bf16[1,128,3584]{2,1,0:T(8,128)(2,1)S(1)} %copy-done, bf16[1,3584,128]{2,1,0:T(8,128)(2,1)S(1)} %copy-done.2, f32[32,8,128]{2,1,0:T(8,128)S(1)} %fusion.42), kind=kOutput, calls=%fused_computation.1 | convolution fusion | flops 470974464 | bytes 5636096 | tf_op jit(solution)/shard_map/sch,dh->scd/dot_general | solution.py:114
  194.2 39.8 %all-to-all-done = bf16[32,8,3584]{2,1,0:T(8,128)(2,1)} async-done(((bf16[32,8,3584]{2,1,0:T(8,128)(2,1)}), bf16[32,8,3584]{2,1,0:T(8,128)(2,1)}, u32[]{:S(2)}, u32[]{:S(2)}) %all-to-all-start) | async-done | bytes 1835040 | tf_op jit(solution)/shard_map/all_to_all | solution.py:86
  234.0 6.2 %all-to-all-start.4 = ((bf16[32,8,3584]{2,1,0:T(8,128)(2,1)}), bf16[32,8,3584]{2,1,0:T(8,128)(2,1)}, u32[]{:S(2)}, u32[]{:S(2)}) async-start(bf16[32,8,3584]{2,1,0:T(8,128)(2,1)} %convolution_convert_fusion.1), calls=%async_computation.4 | async-start | bytes 3670016 | tf_op jit(solution)/shard_map/all_to_all | solution.py:118
  240.2 4.9 %convolution_convert_fusion.2 = bf16[32,8,3584]{2,1,0:T(8,128)(2,1)} fusion(bf16[1,128,3584]{2,1,0:T(8,128)(2,1)S(1)} %copy-done, bf16[32,8,3584]{2,1,0:T(8,128)(2,1)} %all-to-all-done, bf16[1,3584,128]{2,1,0:T(8,128)(2,1)S(1)} %copy-done.2), kind=kOutput, calls=%fused_computation.2 | convolution fusion | flops 470843392 | bytes 5505024 | tf_op jit(solution)/shard_map/sch,hd->scd/dot_general | solution.py:91
  245.1 39.8 %all-to-all-done.4 = bf16[32,8,3584]{2,1,0:T(8,128)(2,1)} async-done(((bf16[32,8,3584]{2,1,0:T(8,128)(2,1)}), bf16[32,8,3584]{2,1,0:T(8,128)(2,1)}, u32[]{:S(2)}, u32[]{:S(2)}) %all-to-all-start.4) | async-done | bytes 1835040 | tf_op jit(solution)/shard_map/all_to_all | solution.py:118
  284.9 6.2 %all-to-all-start.1 = ((bf16[32,8,3584]{2,1,0:T(8,128)(2,1)}), bf16[32,8,3584]{2,1,0:T(8,128)(2,1)}, u32[]{:S(2)}, u32[]{:S(2)}) async-start(bf16[32,8,3584]{2,1,0:T(8,128)(2,1)} %convolution_convert_fusion.2), calls=%async_computation.1 | async-start | bytes 3670016 | tf_op jit(solution)/shard_map/all_to_all | solution.py:94
  292.2 2.9 fusion.7
  295.5 1.8 convert_reduce_fusion
  297.3 0.9 convolution_bitcast_fusion
  299.4 3.8 %collective-permute-start.1 = (bf16[64,3584]{1,0:T(8,128)(2,1)S(1)}, bf16[64,3584]{1,0:T(8,128)(2,1)S(1)}, u32[]{:S(2)}, u32[]{:S(2)}) collective-permute-start(bf16[64,3584]{1,0:T(8,128)(2,1)S(1)} %fusion.1), channel_id=1, source_target_pairs={{480,0},{0,32},{32,64},{64,96},{96,128},{128,160},{160,192},{192,2... | collective-permute-start | bytes 1376264 | tf_op jit(solution)/shard_map/ppermute | solution.py:17
  303.2 32.6 %all-to-all-done.1 = bf16[32,8,3584]{2,1,0:T(8,128)(2,1)} async-done(((bf16[32,8,3584]{2,1,0:T(8,128)(2,1)}), bf16[32,8,3584]{2,1,0:T(8,128)(2,1)}, u32[]{:S(2)}, u32[]{:S(2)}) %all-to-all-start.1) | async-done | bytes 1835040 | tf_op jit(solution)/shard_map/all_to_all | solution.py:94
  335.7 1.8 convert_reduce_fusion.1
  337.6 0.9 fusion
  338.5 3.7 %collective-permute-start = (bf16[64,3584]{1,0:T(8,128)(2,1)S(1)}, bf16[64,3584]{1,0:T(8,128)(2,1)S(1)}, u32[]{:S(2)}, u32[]{:S(2)}) collective-permute-start(bf16[64,3584]{1,0:T(8,128)(2,1)S(1)} %fusion), channel_id=1, source_target_pairs={{480,0},{0,32},{32,64},{64,96},{96,128},{128,160},{160,192},{192,2... | collective-permute-start | bytes 1376264 | tf_op jit(solution)/shard_map/ppermute | solution.py:17
  342.3 16.2 %collective-permute-done = bf16[64,3584]{1,0:T(8,128)(2,1)S(1)} collective-permute-done((bf16[64,3584]{1,0:T(8,128)(2,1)S(1)}, bf16[64,3584]{1,0:T(8,128)(2,1)S(1)}, u32[]{:S(2)}, u32[]{:S(2)}) %collective-permute-start) | collective-permute-done | bytes 458784 | tf_op jit(solution)/shard_map/ppermute | solution.py:17
  358.5 0.8 copy.63
  359.3 0.8 copy.64
  (59 shorter events, 5.9 us)
Async XLA Ops:
  7.2 70.7 %copy-start = (bf16[1,128,3584]{2,1,0:T(8,128)(2,1)S(1)}, bf16[1,128,3584]{2,1,0:T(8,128)(2,1)}, u32[]{:S(2)}) copy-start(bf16[1,128,3584]{2,1,0:T(8,128)(2,1)} %param.15) | copy-start | bytes 2752516
  10.9 11.4 %copy-start.6 = (bf16[1,64,3584]{2,1,0:T(8,128)(2,1)S(1)}, bf16[1,64,3584]{2,1,0:T(8,128)(2,1)}, u32[]{:S(2)}) copy-start(bf16[1,64,3584]{2,1,0:T(8,128)(2,1)} %param.10) | copy-start | bytes 1376260
  10.9 56.0 %all-to-all-start.3 = ((bf16[32,8,3584]{2,1,0:T(8,128)(2,1)}), bf16[32,8,3584]{2,1,0:T(8,128)(2,1)S(1)}, u32[]{:S(2)}, u32[]{:S(2)}) async-start(bf16[32,8,3584]{2,1,0:T(8,128)(2,1)} %bitcast.138), calls=%async_computation.3 | async-start | bytes 3670016 | tf_op jit(solution)/shard_map/all_to_all | solution.py:105
  66.8 1.8 copy-start.3
  68.6 7.1 %copy-start.2 = (bf16[1,3584,128]{2,1,0:T(8,128)(2,1)S(1)}, bf16[1,3584,128]{2,1,0:T(8,128)(2,1)}, u32[]{:S(2)}) copy-start(bf16[1,3584,128]{2,1,0:T(8,128)(2,1)} %param.14) | copy-start | bytes 2752516
  68.6 52.1 %all-to-all-start.2 = ((bf16[32,8,3584]{2,1,0:T(8,128)(2,1)}), bf16[32,8,3584]{2,1,0:T(8,128)(2,1)}, u32[]{:S(2)}, u32[]{:S(2)}) async-start(bf16[32,8,3584]{2,1,0:T(8,128)(2,1)} %bitcast.136), calls=%async_computation.2 | async-start | bytes 3670016 | tf_op jit(solution)/shard_map/all_to_all | solution.py:106
  75.0 101.9 %all-gather.3.cloned.1.call-start = ((), (), s32[]{:S(2)}) async-start(), calls=%async_computation.6 | async-start | bytes 1892352 | tf_op jit(solution)/shard_map/all_gather | solution.py:77
  79.8 47.6 %copy-start.10 = (s32[1,64,8]{1,2,0:T(8,128)S(1)}, s32[1,64,8]{1,2,0:T(8,128)}, u32[]{:S(2)}) copy-start(s32[1,64,8]{1,2,0:T(8,128)} %param.11) | copy-start | bytes 6148
  79.8 97.1 %copy-start.4 = (bf16[1,64,3584]{2,1,0:T(8,128)(2,1)S(1)}, bf16[1,64,3584]{2,1,0:T(8,128)(2,1)}, u32[]{:S(2)}) copy-start(bf16[1,64,3584]{2,1,0:T(8,128)(2,1)} %param.8) | copy-start | bytes 1376260
  120.8 59.8 %all-to-all-start.5 = ((bf16[32,8,3584]{2,1,0:T(8,128)(2,1)}), bf16[32,8,3584]{2,1,0:T(8,128)(2,1)}, u32[]{:S(2)}, u32[]{:S(2)}) async-start(bf16[32,8,3584]{2,1,0:T(8,128)(2,1)} %convolution_convert_fusion), calls=%async_computation.5 | async-start | bytes 3670016 | tf_op jit(solution)/shard_map/all_to_all | solution.py:119
  180.3 1.6 copy-start.8
  182.0 52.0 %all-to-all-start = ((bf16[32,8,3584]{2,1,0:T(8,128)(2,1)}), bf16[32,8,3584]{2,1,0:T(8,128)(2,1)}, u32[]{:S(2)}, u32[]{:S(2)}) async-start(bf16[32,8,3584]{2,1,0:T(8,128)(2,1)} %bitcast.137), calls=%async_computation | async-start | bytes 3670016 | tf_op jit(solution)/shard_map/all_to_all | solution.py:86
  234.0 50.9 %all-to-all-start.4 = ((bf16[32,8,3584]{2,1,0:T(8,128)(2,1)}), bf16[32,8,3584]{2,1,0:T(8,128)(2,1)}, u32[]{:S(2)}, u32[]{:S(2)}) async-start(bf16[32,8,3584]{2,1,0:T(8,128)(2,1)} %convolution_convert_fusion.1), calls=%async_computation.4 | async-start | bytes 3670016 | tf_op jit(solution)/shard_map/all_to_all | solution.py:118
  245.1 46.0 %copy-start.7 = (s32[1,64,8]{1,2,0:T(8,128)S(1)}, s32[1,64,8]{1,2,0:T(8,128)}, u32[]{:S(2)}) copy-start(s32[1,64,8]{1,2,0:T(8,128)} %param.12) | copy-start | bytes 6148
  245.1 46.1 %copy-start.1 = (bf16[1,3584,256]{2,1,0:T(8,128)(2,1)S(1)}, bf16[1,3584,256]{2,1,0:T(8,128)(2,1)}, u32[]{:S(2)}) copy-start(bf16[1,3584,256]{2,1,0:T(8,128)(2,1)} %all-gather.3.cloned.1.call-done) | copy-start | bytes 5505028
  245.1 46.1 %copy-start.5 = (bf16[1,64,3584]{2,1,0:T(8,128)(2,1)S(1)}, bf16[1,64,3584]{2,1,0:T(8,128)(2,1)}, u32[]{:S(2)}) copy-start(bf16[1,64,3584]{2,1,0:T(8,128)(2,1)} %param.9) | copy-start | bytes 1376260
  284.9 50.8 %all-to-all-start.1 = ((bf16[32,8,3584]{2,1,0:T(8,128)(2,1)}), bf16[32,8,3584]{2,1,0:T(8,128)(2,1)}, u32[]{:S(2)}, u32[]{:S(2)}) async-start(bf16[32,8,3584]{2,1,0:T(8,128)(2,1)} %convolution_convert_fusion.2), calls=%async_computation.1 | async-start | bytes 3670016 | tf_op jit(solution)/shard_map/all_to_all | solution.py:94
  299.4 38.2 %copy-start.9 = (f32[4,64]{1,0:T(4,128)S(1)}, f32[4,64]{1,0:T(4,128)}, u32[]{:S(2)}) copy-start(f32[4,64]{1,0:T(4,128)} %copy-done.8) | copy-start | bytes 3076
  299.4 38.2 %copy-start.11 = (f32[64,4]{0,1:T(4,128)S(1)}, f32[64,4]{0,1:T(4,128)}, u32[]{:S(2)}) copy-start(f32[64,4]{0,1:T(4,128)} %get-tuple-element.4) | copy-start | bytes 3076
  299.4 42.9 %collective-permute-start.1 = (bf16[64,3584]{1,0:T(8,128)(2,1)S(1)}, bf16[64,3584]{1,0:T(8,128)(2,1)S(1)}, u32[]{:S(2)}, u32[]{:S(2)}) collective-permute-start(bf16[64,3584]{1,0:T(8,128)(2,1)S(1)} %fusion.1), channel_id=1, source_target_pairs={{480,0},{0,32},{32,64},{64,96},{96,128},{128,160},{160,192},{192,2... | collective-permute-start | bytes 1376264 | tf_op jit(solution)/shard_map/ppermute | solution.py:17
  338.5 20.0 %collective-permute-start = (bf16[64,3584]{1,0:T(8,128)(2,1)S(1)}, bf16[64,3584]{1,0:T(8,128)(2,1)S(1)}, u32[]{:S(2)}, u32[]{:S(2)}) collective-permute-start(bf16[64,3584]{1,0:T(8,128)(2,1)S(1)} %fusion), channel_id=1, source_target_pairs={{480,0},{0,32},{32,64},{64,96},{96,128},{128,160},{160,192},{192,2... | collective-permute-start | bytes 1376264 | tf_op jit(solution)/shard_map/ppermute | solution.py:17
Sparse Core Ops, SparseCore 0:
  79.2 97.6 all-gather.2
where the time goes:
time: 368 us; the launch traced here: 367 us
  waiting for transfers between devices  264 us (72%)
  starting transfers between devices  51.6 us (14%)
  matrix products  24.7 us (7%)
  between operations  14.3 us (4%)
  local copies, waits for them, and re-layouts  6.89 us (2%)
  other arithmetic  5.39 us (1%)
    all_gather x1, waiting for transfers between devices, on_device(): lax.all_gather(router_weight[0], 'expert', axis=0, tiled=True)  49.4 us
    all_to_all x1, waiting for transfers between devices, on_device(): lax.all_to_all(outgoing_bwd, 'expert', split_axis=0, concat_axis=0, tiled...  44.4 us
    all_to_all x1, waiting for transfers between devices, on_device(): lax.all_to_all(outgoing_cot, 'expert', split_axis=0, concat_axis=0, tiled...  41 us
    all_to_all x1, waiting for transfers between devices, on_device(): lax.all_to_all(outgoing_fwd, 'expert', split_axis=0, concat_axis=0, tiled...  39.8 us
    all_to_all x1, waiting for transfers between devices, on_device(): lax.all_to_all(grad_rows, 'expert', split_axis=0, concat_axis=0, tiled=True)  39.8 us
    all_to_all x1, waiting for transfers between devices, on_device(): lax.all_to_all(shares_fwd, 'expert', split_axis=0, concat_axis=0, tiled=T...  32.6 us
    ppermute x2, waiting for transfers between devices, passed_along(): return lax.ppermute(block, axis, route)  16.2 us
    all_to_all x1, starting transfers between devices, on_device(): lax.all_to_all(outgoing_bwd, 'expert', split_axis=0, concat_axis=0, tiled...  11.3 us
  transfers between devices with their start and end apart: 9, of which 7 were waited for; matrix products, arithmetic and copies ran while one was open for 8% of the time, Pallas kernels for 0%

commit v1 on v0

v1 whole, which is shorter than its diff:
```python
import functools

import jax
import jax.numpy as jnp
from jax import lax
from jax.experimental import pallas as pl
from jax.experimental.pallas import tpu as pltpu
from jax.sharding import PartitionSpec as P

MESH = pl.DeviceIdType.MESH
D = 3584
HALF = D // 2
EXPERTS = 256
CAP = 8
FLIGHT = 4
SLOTS = FLIGHT * CAP
TOK = 64
HID = 128
WROWS = 112
NY = 8
SECTIONS = 16
ROUTE_SCALE = 2.5
HIGHEST = lax.Precision.HIGHEST
F32 = jnp.float32
BF16 = jnp.bfloat16
OFFSETS = (2, -1, -3)


def across(a, b):
    return lax.dot_general(a, b, (((1,), (1,)), ((), ())), preferred_element_type=F32)


def dot(a, b):
    return jnp.dot(a, b, preferred_element_type=F32)


def exact(a, b):
    return jnp.dot(a, b, preferred_element_type=F32, precision=HIGHEST)


def sigmoid(v):
    return 1.0 / (1.0 + jnp.exp(-v))


def chosen_mask(routes_ref):
    ids = lax.broadcasted_iota(jnp.int32, (TOK, EXPERTS), 1)
    mask = jnp.zeros((TOK, EXPERTS), F32)
    for k in range(routes_ref.shape[1]):
        mask = mask + jnp.where(routes_ref[:, k : k + 1] == ids, 1.0, 0.0)
    return mask


def to_slots(columns):
    lane = lax.broadcasted_iota(jnp.int32, (TOK, 128), 1)
    out = jnp.zeros((TOK, 128), F32)
    for e in range(FLIGHT):
        inside = (lane >= e * CAP) & (lane < (e + 1) * CAP)
        out = out + jnp.where(inside, jnp.broadcast_to(columns[:, e : e + 1], (TOK, 128)), 0.0)
    return out


def slot_select(mask):
    member = to_slots(mask)
    row = lax.broadcasted_iota(jnp.int32, (TOK, TOK), 0)
    col = lax.broadcasted_iota(jnp.int32, (TOK, TOK), 1)
    below = jnp.where(col < row, 1.0, 0.0).astype(BF16)
    placing = dot(below, member.astype(BF16))
    lane = lax.broadcasted_iota(jnp.int32, (TOK, 128), 1)
    slot = (lane % CAP).astype(F32)
    return jnp.where(placing == slot, member, 0.0)


def kernel(
    xf_hbm, xb_hbm, g_hbm, rf_ref, rb_ref, w_hbm, up_hbm, dn_hbm,
    of_ref, ob_ref,
    xf, xb, g, up, dn, wg, pb, pf, pfx, rows_b, rows_f,
    acc1, acc2, send_dot, got_dot, out_b, out_f, rx_b, rx_f,
    ps_b, ps_f, pr_b, pr_f, fs_b, fs_f, fin_b, fin_f,
    msg, msg_in, rr, rr_in,
    lsem, ssem, rsem,
):
    p = lax.axis_index("pipe")
    me = lax.axis_index("expert")
    y = me // 4
    xh = (me // 2) % 2
    c = me % 2
    e = y // 2
    sig = 1 - 2 * (y % 2)
    nxt = (p + 1) % SECTIONS
    prv = (p + SECTIONS - 1) % SECTIONS

    def at(yy, xx=None, cc=None, pp=None):
        xx = xh if xx is None else xx
        cc = c if cc is None else cc
        return (p if pp is None else pp, (yy * 2 + xx) * 2 + cc)

    def shift(off):
        return (y + NY + sig * off) % NY

    def slot_y(s):
        return shift(-s) if s < 4 else shift(s - 3)

    sib = at(y, cc=1 - c)
    xpart = at(y, xx=1 - xh)
    pair = at(shift(1))

    bar = pltpu.get_barrier_semaphore()

    def greet(dev):
        pl.semaphore_signal(bar, inc=1, device_id=dev, device_id_type=MESH)

    for s in range(8):
        if s:
            greet(at(slot_y(s)))
        greet(at(slot_y(s), xx=1 - xh))
    greet(sib)
    greet(at(y, pp=prv))
    greet(at(y, xx=1 - xh, pp=prv))

    nsem = [0]
    nlocal = [0]
    sends = []

    def ids(n):
        first = nsem[0]
        nsem[0] += n
        return first

    def local(src, dst):
        cp = pltpu.make_async_copy(src, dst, lsem.at[nlocal[0]])
        nlocal[0] += 1
        cp.start()
        return cp

    def push(src, dst, dev, s_id, r_id=None):
        cp = pltpu.make_async_remote_copy(
            src_ref=src, dst_ref=dst, send_sem=ssem.at[s_id],
            recv_sem=rsem.at[s_id if r_id is None else r_id],
            device_id=dev, device_id_type=MESH,
        )
        cp.start()
        sends.append(cp)

    def got(dst, r_id):
        pltpu.make_async_remote_copy(
            src_ref=dst, dst_ref=dst, send_sem=ssem.at[0], recv_sem=rsem.at[r_id],
            device_id=sib, device_id_type=MESH,
        ).wait_recv()

    l_xb = local(xb_hbm, xb)
    l_g = local(g_hbm, g)
    l_xf = local(xf_hbm, xf)
    l_up = local(up_hbm, up.at[:, pl.ds(0, HID)])
    l_dn = local(dn_hbm, dn.at[pl.ds(0, HID)])
    my_w = y * 2 + xh
    l_w = local(w_hbm, wg.at[my_w, c])

    mask_b = chosen_mask(rb_ref)
    mask_f = chosen_mask(rf_ref)
    sel_b = slot_select(mask_b)
    sel_f = slot_select(mask_f)
    pick_b = sel_b.T[:SLOTS].astype(BF16)
    pick_f = sel_f.T[:SLOTS].astype(BF16)

    l_xb.wait()
    l_g.wait()

    @pl.loop(0, 7)
    def _(i):
        cols = pl.ds(pl.multiple_of(i * 512, 512), 512)
        a = dot(pick_b, xb[:, cols]).reshape(FLIGHT, CAP, 512)
        b = dot(pick_b, g[:, cols]).reshape(FLIGHT, CAP, 512)
        pb[:, :, cols] = jnp.concatenate([a, b], axis=1).astype(BF16)

    l_xf.wait()

    @pl.loop(0, 7)
    def _(i):
        lo = pl.ds(pl.multiple_of(i * 256, 256), 256)
        hi = pl.ds(pl.multiple_of(HALF + i * 256, 256), 256)
        a = dot(pick_f, xf[:, lo]).reshape(FLIGHT, CAP, 256)
        b = dot(pick_f, xf[:, hi]).reshape(FLIGHT, CAP, 256)
        pf[:, :, lo] = jnp.concatenate([a, b], axis=1).astype(BF16)

    pl.semaphore_wait(bar, 18)

    by = ids(8)
    bx = ids(8)
    for off in OFFSETS:
        t = shift(off)
        push(pb.at[t // 2], rows_b.at[0, abs(off)], at(t), by + abs(off))
    push(pb.at[e], rows_b.at[0, 4], pair, by + 4)
    push(pb.at[e], rows_b.at[1, 0], xpart, bx)
    l_b0 = local(pb.at[e], rows_b.at[0, 0])

    fx = ids(1)
    push(pf, pfx, xpart, fx)

    su = ids(2)
    push(up_hbm, up.at[:, pl.ds(HID, HID)], sib, su)
    push(dn_hbm, dn.at[pl.ds(HID, HID)], sib, su + 1)
    wx = ids(1)
    push(w_hbm, wg.at[my_w, c], xpart, wx)

    fy = [ids(8), ids(8)]

    def send_f(col, src):
        for off in OFFSETS:
            t = shift(off)
            push(src.at[t // 2], rows_f.at[col, abs(off)], at(t), fy[col] + abs(off))
        push(src.at[e], rows_f.at[col, 4], pair, fy[col] + 4)
        return local(src.at[e], rows_f.at[col, 0])

    def hand_b(s):
        got(rows_b.at[0, s], by + s)
        if s < 4:
            push(rows_b.at[0, s], rows_b.at[0, 4 + s], pair, by + 4 + s)
        push(rows_b.at[0, s], rows_b.at[1, s], xpart, bx + s)

    def hand_f(col, s):
        got(rows_f.at[col, s], fy[col] + s)
        push(rows_f.at[col, s], rows_f.at[col, 4 + s], pair, fy[col] + 4 + s)

    l_f0 = send_f(0, pf)
    hand_b(1)
    hand_b(4)
    got(pfx, fx)
    l_f1 = send_f(1, pfx)
    for s in (2, 5, 3, 6, 7):
        hand_b(s)
    for s in (1, 2, 3):
        hand_f(0, s)
        hand_f(1, s)

    up_dev, down_dev = at((y + 1) % NY), at((y + NY - 1) % NY)
    wr = ids(16)
    l_w.wait()
    got(wg.at[y * 2 + (1 - xh), c], wx)

    def ring(step):
        yu = (y + NY - step) % NY
        yd = (y + step) % NY
        for xx in range(2):
            if step < 3 or xx == 0:
                push(wg.at[yu * 2 + xx, c], wg.at[yu * 2 + xx, c], up_dev, wr + step * 2 + xx)
            if step < 3 or xx == 1:
                push(wg.at[yd * 2 + xx, c], wg.at[yd * 2 + xx, c], down_dev, wr + 8 + step * 2 + xx)

    def ring_got(step):
        yu = (y + NY - step - 1) % NY
        yd = (y + step + 1) % NY
        for xx in range(2):
            if step < 3 or xx == 0:
                got(wg.at[yu * 2 + xx, c], wr + step * 2 + xx)
            if step < 3 or xx == 1:
                got(wg.at[yd * 2 + xx, c], wr + 8 + step * 2 + xx)

    ring(0)

    l_b0.wait()
    l_up.wait()
    l_dn.wait()
    got(up.at[:, pl.ds(HID, HID)], su)
    got(dn.at[pl.ds(HID, HID)], su + 1)
    for s in range(8):
        got(rows_b.at[1, s], bx + s)

    acc1[...] = jnp.zeros_like(acc1)
    acc2[...] = jnp.zeros_like(acc2)

    @pl.loop(0, 7)
    def _(i):
        cols = pl.ds(pl.multiple_of(i * 512, 512), 512)
        r = rows_b[:, :, :, cols].reshape(256, 512)
        acc1[...] += dot(r, up[cols, :])
        acc2[...] += across(r, dn[:, cols])

    pre = acc1[...].reshape(16, 16, 256)[:, :CAP].reshape(128, 256)
    act_grad = acc2[...].reshape(16, 16, 256)[:, CAP:].reshape(128, 256)
    s = sigmoid(pre)
    act = (pre * s).astype(BF16).astype(F32)
    dots = jnp.sum(act * act_grad, axis=1, keepdims=True)
    send_dot[...] = jnp.broadcast_to(dots, (128, 128)).reshape(2, 8, CAP, 128)
    mine = e * 4 + (y % 2) * 2 + xh
    dt_s = ids(16)
    dt_r = ids(16)
    for col in range(2):
        for k in range(8):
            if col == 0 and k == 0:
                continue
            dev = at(slot_y(k), xx=xh if col == 0 else 1 - xh)
            push(send_dot.at[col, k], got_dot.at[mine], dev, dt_s + col * 8 + k, dt_r + mine)
    l_dot = local(send_dot.at[0, 0], got_dot.at[mine])

    pre_grad = (act_grad * (s * (1.0 + pre * (1.0 - s)))).astype(BF16)

    @pl.loop(0, 7)
    def _(i):
        lo = pl.ds(pl.multiple_of(i * 256, 256), 256)
        hi = pl.ds(pl.multiple_of(HALF + i * 256, 256), 256)
        a = across(pre_grad, up[lo, :]).reshape(2, 8, CAP, 256)
        b = across(pre_grad, up[hi, :]).reshape(2, 8, CAP, 256)
        out_b[:, :, :, lo] = jnp.concatenate([a, b], axis=2).astype(BF16)

    def send_back(out, rx, first):
        for half in (1, 0):
            part = pl.ds(half * 4, 4)
            for col in range(2):
                dev = at(y, xx=xh if col == 0 else 1 - xh, pp=nxt)
                push(out.at[col, part], rx.at[col, part], dev, first + half * 2 + col)

    rb = ids(4)
    send_back(out_b, rx_b, rb)
    ring_got(0)
    ring(1)

    l_f0.wait()
    l_f1.wait()
    for col in range(2):
        for k in range(4, 8):
            got(rows_f.at[col, k], fy[col] + k)
    acc1[...] = jnp.zeros_like(acc1)
    acc2[...] = jnp.zeros_like(acc2)

    @pl.loop(0, 7)
    def _(i):
        lo = pl.ds(pl.multiple_of(i * 256, 256), 256)
        hi = pl.ds(pl.multiple_of(HALF + i * 256, 256), 256)
        r = rows_f[:, :, :, lo].reshape(256, 256)
        acc1[...] += dot(r, up[lo, :])
        acc2[...] += dot(r, up[hi, :])

    pre_f = (
        acc1[...].reshape(16, 16, 256)[:, :CAP] + acc2[...].reshape(16, 16, 256)[:, CAP:]
    ).reshape(128, 256)
    act_f = (pre_f * sigmoid(pre_f)).astype(BF16)

    @pl.loop(0, 7)
    def _(i):
        lo = pl.ds(pl.multiple_of(i * 256, 256), 256)
        hi = pl.ds(pl.multiple_of(HALF + i * 256, 256), 256)
        a = dot(act_f, dn[:, lo]).reshape(2, 8, CAP, 256)
        b = dot(act_f, dn[:, hi]).reshape(2, 8, CAP, 256)
        out_f[:, :, :, lo] = jnp.concatenate([a, b], axis=2).astype(BF16)

    rf = ids(4)
    send_back(out_f, rx_f, rf)
    ring_got(1)
    ring(2)

    def to_pair(rx, ps, pr, first, pid):
        got(rx.at[0, pl.ds(4, 4)], first + 2)
        got(rx.at[1, pl.ds(4, 4)], first + 3)

        @pl.loop(0, 4)
        def _(k):
            ps[k] = (rx[0, 4 + k].astype(F32) + rx[1, 4 + k].astype(F32)).astype(BF16)

        push(ps, pr, pair, pid)

    def to_home(rx, pr, fs, fin, first, pid, s_id, r_id):
        got(rx.at[0, pl.ds(0, 4)], first)
        got(rx.at[1, pl.ds(0, 4)], first + 1)
        got(pr, pid)

        @pl.loop(0, 4)
        def _(k):
            fs[k] = (rx[0, k].astype(F32) + rx[1, k].astype(F32) + pr[k].astype(F32)).astype(BF16)

        for k in range(1, 4):
            push(fs.at[k], fin.at[e], at(shift(-k)), s_id + k, r_id + e)
        return local(fs.at[0], fin.at[e])

    pid_b, pid_f = ids(1), ids(1)
    hs_b, hr_b, hs_f, hr_f = ids(4), ids(4), ids(4), ids(4)
    to_pair(rx_b, ps_b, pr_b, rb, pid_b)
    ring_got(2)
    ring(3)
    l_hb = to_home(rx_b, pr_b, fs_b, fin_b, rb, pid_b, hs_b, hr_b)
    ring_got(3)
    ws = ids(1)
    push(wg.at[:, c], wg.at[:, c], sib, ws)
    to_pair(rx_f, ps_f, pr_f, rf, pid_f)
    got(wg.at[:, 1 - c], ws)

    def scores(x):
        total = jnp.zeros((TOK, EXPERTS), F32)
        for i in range(4):
            w = wg[pl.ds(4 * i, 4)].reshape(896, EXPERTS)
            total = total + dot(x[:, pl.ds(896 * i, 896)], w)
        return sigmoid(total)

    score_f = scores(xf)
    score_b = scores(xb)
    sum_f = jnp.sum(mask_f * score_f, axis=1, keepdims=True)
    sum_b = jnp.sum(mask_b * score_b, axis=1, keepdims=True)
    msg[0] = sel_f * to_slots(ROUTE_SCALE * score_f / sum_f)
    msg[1] = sel_b * to_slots(ROUTE_SCALE * score_b / sum_b)
    seen = jnp.zeros((TOK, 1), F32)
    firsts = []
    for k in range(FLIGHT):
        here = mask_b[:, k : k + 1]
        firsts.append(here * (1.0 - seen))
        seen = jnp.maximum(seen, here)
    lane = lax.broadcasted_iota(jnp.int32, (TOK, 128), 1)
    first = jnp.zeros((TOK, 128), F32)
    for k in range(FLIGHT):
        inside = (lane >= k * CAP) & (lane < (k + 1) * CAP)
        first = first + jnp.where(inside, jnp.broadcast_to(firsts[k], (TOK, 128)), 0.0)
    once = sel_b * first
    msg[2] = once
    mg = ids(1)
    push(msg, msg_in, at(y, pp=nxt), mg)

    l_dot.wait()
    for k in range(1, 16):
        other = (mine + k) % 16
        got(got_dot.at[other], dt_r + other)
    all_dots = got_dot[...].reshape(FLIGHT, 4, CAP, 128)
    slot_dots = (all_dots[:, 0] + all_dots[:, 1] + all_dots[:, 2] + all_dots[:, 3]).reshape(SLOTS, 128)
    slot_row = lax.broadcasted_iota(jnp.int32, (SLOTS, EXPERTS), 0)
    slot_col = lax.broadcasted_iota(jnp.int32, (SLOTS, EXPERTS), 1)
    by_expert = jnp.where(
        slot_row // CAP == slot_col, jnp.broadcast_to(slot_dots[:, 0:1], (SLOTS, EXPERTS)), 0.0
    )
    gate_grad = exact(sel_b[:, :SLOTS], by_expert)
    weighted = jnp.sum(gate_grad * score_b, axis=1, keepdims=True) / sum_b
    pick_grad = ROUTE_SCALE / sum_b * (gate_grad - weighted)
    logit_grad = (mask_b * pick_grad * score_b * (1.0 - score_b)).astype(BF16)
    packed = dot(once.T[:SLOTS].astype(BF16), logit_grad).astype(BF16)
    for i in range(4):
        w = wg[pl.ds(4 * i, 4)].reshape(896, EXPERTS)
        rr[:, pl.ds(896 * i, 896)] = across(packed, w).astype(BF16)
    rid = ids(1)
    push(rr, rr_in, at(y, pp=nxt), rid)

    l_hf = to_home(rx_f, pr_f, fs_f, fin_f, rf, pid_f, hs_f, hr_f)

    got(msg_in, mg)
    l_hb.wait()
    for k in range(1, 4):
        got(fin_b.at[(e + k) % 4], hr_b + (e + k) % 4)
    got(rr_in, rid)
    gate_b = msg_in[1][:, :SLOTS]
    once_in = msg_in[2][:, :SLOTS].astype(BF16)

    @pl.loop(0, 7)
    def _(i):
        lo = pl.ds(pl.multiple_of(i * 256, 256), 256)
        hi = pl.ds(pl.multiple_of(HALF + i * 256, 256), 256)
        t = fin_b[:, :, lo].astype(F32)
        a = exact(gate_b, t[:, :CAP].reshape(SLOTS, 256)) + dot(once_in, rr_in[:, lo])
        b = exact(gate_b, t[:, CAP:].reshape(SLOTS, 256)) + dot(once_in, rr_in[:, hi])
        ob_ref[:, lo] = a.astype(BF16)
        ob_ref[:, hi] = b.astype(BF16)

    l_hf.wait()
    for k in range(1, 4):
        got(fin_f.at[(e + k) % 4], hr_f + (e + k) % 4)
    gate_f = msg_in[0][:, :SLOTS]

    @pl.loop(0, 7)
    def _(i):
        lo = pl.ds(pl.multiple_of(i * 256, 256), 256)
        hi = pl.ds(pl.multiple_of(HALF + i * 256, 256), 256)
        t = fin_f[:, :, lo].astype(F32)
        of_ref[:, lo] = exact(gate_f, t[:, :CAP].reshape(SLOTS, 256)).astype(BF16)
        of_ref[:, hi] = exact(gate_f, t[:, CAP:].reshape(SLOTS, 256)).astype(BF16)

    for cp in sends:
        cp.wait_send()


N_SEM = 160


def on_device(xf, xb, g, rf, rb, w, up, dn):
    vm = pltpu.VMEM
    scratch = [
        vm((TOK, D), BF16), vm((TOK, D), BF16), vm((TOK, D), BF16),
        vm((D, 2 * HID), BF16), vm((2 * HID, D), BF16), vm((16, 2, WROWS, EXPERTS), BF16),
        vm((FLIGHT, 16, D), BF16), vm((FLIGHT, 16, HALF), BF16), vm((FLIGHT, 16, HALF), BF16),
        vm((2, 8, 16, D), BF16), vm((2, 8, 16, HALF), BF16),
        vm((256, 256), F32), vm((256, 256), F32),
        vm((2, 8, CAP, 128), F32), vm((16, CAP, 128), F32),
        vm((2, 8, 16, HALF), BF16), vm((2, 8, 16, HALF), BF16),
        vm((2, 8, 16, HALF), BF16), vm((2, 8, 16, HALF), BF16),
        vm((4, 16, HALF), BF16), vm((4, 16, HALF), BF16),
        vm((4, 16, HALF), BF16), vm((4, 16, HALF), BF16),
        vm((4, 16, HALF), BF16), vm((4, 16, HALF), BF16),
        vm((4, 16, HALF), BF16), vm((4, 16, HALF), BF16),
        vm((3, TOK, 128), F32), vm((3, TOK, 128), F32),
        vm((SLOTS, D), BF16), vm((SLOTS, D), BF16),
        pltpu.SemaphoreType.DMA((16,)),
        pltpu.SemaphoreType.DMA((N_SEM,)),
        pltpu.SemaphoreType.DMA((N_SEM,)),
    ]
    hbm = pl.BlockSpec(memory_space=pl.ANY)
    vmem = pl.BlockSpec(memory_space=pltpu.VMEM)
    of, ob = pl.pallas_call(
        kernel,
        out_shape=[jax.ShapeDtypeStruct((TOK, D), BF16)] * 2,
        in_specs=[hbm, hbm, hbm, vmem, vmem, hbm, hbm, hbm],
        out_specs=[vmem, vmem],
        scratch_shapes=scratch,
        compiler_params=pltpu.CompilerParams(
            collective_id=0, has_side_effects=True, vmem_limit_bytes=60 * 2**20
        ),
        cost_estimate=pl.CostEstimate(flops=2 * 10**9, bytes_accessed=6 * 10**6, transcendentals=10**5),
        name="expert_layer",
    )(xf[0], xb[0], g[0], rf[0], rb[0], w[0], up[0], dn[0])
    return of[None], ob[None]


def solution(mesh):
    rows = P("pipe", "expert", None)
    return jax.shard_map(
        on_device,
        mesh=mesh,
        in_specs=(rows, rows, rows, rows, rows, rows, P("pipe", None, "expert"), rows),
        out_specs=(rows, rows),
        check_vma=False,
    )
```

time: 368 us -> 110 us (0.30)
  waiting for transfers between devices: 264 us -> 0 us
  Pallas kernels: 0 us -> 103 us
  starting transfers between devices: 51.6 us -> 0 us
  matrix products: 24.7 us -> 0 us
  between operations: 14.3 us -> 0.66 us
  other arithmetic: 5.39 us -> 0 us
    all_to_all x6 -> x0, waiting for transfers between devices: 198 us -> none  [the longest x1 44.4 us: on_device(): lax.all_to_all(outgoing_bwd, 'expert', split_axis=0, concat_axis=0, tiled...]
    pallas_call x0 -> x1, Pallas kernels: none -> 103 us  [on_device(): pl.pallas_call(kernel, out_shape=[jax.ShapeDtypeStruct((TOK, D), BF16)] *...]
    all_gather x1 -> x0, waiting for transfers between devices: 49.4 us -> none  [on_device(): lax.all_gather(router_weight[0], 'expert', axis=0, tiled=True)]
    all_to_all x6 -> x0, starting transfers between devices: 44.1 us -> none  [the longest x1 11.3 us: on_device(): lax.all_to_all(outgoing_bwd, 'expert', split_axis=0, concat_axis=0, tiled...]
    dot_general x17 -> x0, matrix products: 24.7 us -> none  [the longest x2 6.8 us: on_device(): jnp.einsum('sch,hd->scd', activation, down_local, preferred_element_type=...]
    ppermute x2 -> x0, waiting for transfers between devices: 16.2 us -> none  [passed_along(): return lax.ppermute(block, axis, route)]
    ppermute x2 -> x0, starting transfers between devices: 7.52 us -> none  [passed_along(): return lax.ppermute(block, axis, route)]
    reduce_sum x6 -> x0, other arithmetic: 4.52 us -> none  [the longest x2 3.61 us: slice_sum(): jnp.sum(returned.reshape((flight, SLICES) + returned.shape[1:]).astype(jn...]
  transfers between devices with their start and end apart: 9 -> 0, of which waited for: 7 -> 0; matrix products, arithmetic and copies ran while one was open for 8% -> 0% of each run, Pallas kernels for 0% -> 0%
where the time goes in v1:
time: 110 us; the launch traced here: 109 us
  Pallas kernels  103 us (94%)
  local copies, waits for them, and re-layouts  4.72 us (4%)
    pallas_call x1, Pallas kernels, on_device(): pl.pallas_call(kernel, out_shape=[jax.ShapeDtypeStruct((TOK, D), BF16)] *...  103 us
    unnamed x10, local copies, waits for them, and re-layouts  4.72 us

profile of v1, /device:TPU:1, one launch (start us, length us, event | category | flops | bytes accessed | tf_op | source)
XLA Modules:
  0.0 108.7 jit_solution(3567663931997312468)
XLA Ops:
  0.6 0.0 copy-start.1
  0.6 0.7 copy-done.1
  1.3 0.0 copy-start.2
  1.3 0.7 copy.10
  2.0 0.0 copy-done.2
  2.0 0.7 copy.11
  2.7 103.3 %expert_layer.1 = (bf16[64,3584]{1,0:T(8,128)(2,1)}, bf16[64,3584]{1,0:T(8,128)(2,1)}) custom-call(bf16[64,3584]{1,0:T(8,128)(2,1)} %bitcast.16, bf16[64,3584]{1,0:T(8,128)(2,1)} %bitcast.17, bf16[64,3584]{1,0:T(8,128)(2,1)} %bitcast.18, s32[64,8]{1,0:T(8,128)} %bitcast.12, s32[64,8]{1,0:T(8,128)} %bitcast.13, bf16[112,256]{1,0:T(8,128)(2,1)} %bitcast.19, ...), custom_call_target="tpu_custom_call" | custom-call | flops 2000000000 | bytes 6000000 | tf_op jit(solution)/shard_map/expert_layer/pallas_call | solution.py:500
  106.1 0.0 copy-start
  106.1 1.9 %copy.14 = bf16[1,64,3584]{2,1,0:T(8,128)(2,1)} copy(bf16[1,64,3584]{2,1,0:T(8,128)(2,1)} %bitcast.11) | data formatting | bytes 917504
  107.9 0.0 copy-done
  107.9 0.8 copy.15
Async XLA Ops:
  0.6 0.7 copy-start.1
  1.3 0.7 copy-start.2
  106.1 1.9 %copy-start = (bf16[64,3584]{1,0:T(8,128)(2,1)S(1)}, bf16[64,3584]{1,0:T(8,128)(2,1)}, u32[]{:S(2)}) copy-start(bf16[64,3584]{1,0:T(8,128)(2,1)} %get-tuple-element.5) | copy-start | bytes 1376260

commit v2 on v1

v2 whole, which is shorter than its diff:
```python
import functools

import jax
import jax.numpy as jnp
from jax import lax
from jax.experimental import pallas as pl
from jax.experimental.pallas import tpu as pltpu
from jax.sharding import PartitionSpec as P

MESH = pl.DeviceIdType.MESH
D = 3584
HALF = D // 2
PART = HALF // 2
EXPERTS = 256
CAP = 8
FLIGHT = 4
SLOTS = FLIGHT * CAP
TOK = 64
HID = 128
WROWS = 112
NY = 8
DN = 4
SECTIONS = 16
ROUTE_SCALE = 2.5
HIGHEST = lax.Precision.HIGHEST
F32 = jnp.float32
BF16 = jnp.bfloat16
OFFSETS = (-1, 2, -3)


def across(a, b):
    return lax.dot_general(a, b, (((1,), (1,)), ((), ())), preferred_element_type=F32)


def dot(a, b):
    return jnp.dot(a, b, preferred_element_type=F32)


def exact(a, b):
    return jnp.dot(a, b, preferred_element_type=F32, precision=HIGHEST)


def sigmoid(v):
    return 1.0 / (1.0 + jnp.exp(-v))


def chosen_mask(routes_ref):
    wide = jnp.concatenate([routes_ref[...].astype(F32)] * 2, axis=1)
    routes = wide.T[:TOK]
    ids = lax.broadcasted_iota(jnp.int32, (TOK, EXPERTS), 1).astype(F32)
    mask = jnp.zeros((TOK, EXPERTS), F32)
    for k in range(routes_ref.shape[0]):
        mask = mask + jnp.where(routes[:, k : k + 1] == ids, 1.0, 0.0)
    return mask


def two_parts(v):
    high = v.astype(BF16)
    return high, (v - high.astype(F32)).astype(BF16)


def to_slots(columns):
    lane = lax.broadcasted_iota(jnp.int32, (TOK, 128), 1)
    out = jnp.zeros((TOK, 128), F32)
    for e in range(FLIGHT):
        inside = (lane >= e * CAP) & (lane < (e + 1) * CAP)
        out = out + jnp.where(inside, jnp.broadcast_to(columns[:, e : e + 1], (TOK, 128)), 0.0)
    return out


def slot_select(mask):
    member = to_slots(mask)
    row = lax.broadcasted_iota(jnp.int32, (TOK, TOK), 0)
    col = lax.broadcasted_iota(jnp.int32, (TOK, TOK), 1)
    below = jnp.where(col < row, 1.0, 0.0).astype(BF16)
    placing = dot(below, member.astype(BF16))
    lane = lax.broadcasted_iota(jnp.int32, (TOK, 128), 1)
    slot = (lane % CAP).astype(F32)
    return jnp.where(placing == slot, member, 0.0)


def kernel(
    xf_hbm, xb_hbm, g_hbm, rf_ref, rb_ref, w_hbm, up_hbm, dn_hbm,
    of_ref, ob_ref,
    xf, xb, g, up, dn, wg, pb, pf, rows_b, rows_f,
    pre_b, grad_b, pre_f, send_dot, got_dot, out_b, out_f,
    pr_b, pr_f, fs_b, fs_f, fin_b, fin_f,
    msg, msg_in, lg, lg_in,
    lsem, ssem, rsem,
):
    p = lax.axis_index("pipe")
    me = lax.axis_index("expert")
    y = me // 4
    xh = (me // 2) % 2
    c = me % 2
    e = y // 2
    sig = 1 - 2 * (y % 2)
    nxt = (p + 1) % SECTIONS
    prv = (p + SECTIONS - 1) % SECTIONS

    def at(yy, xx=None, cc=None, pp=None):
        xx = xh if xx is None else xx
        cc = c if cc is None else cc
        return (p if pp is None else pp, (yy * 2 + xx) * 2 + cc)

    def shift(off):
        return (y + NY + sig * off) % NY

    def slot_y(s):
        return shift(-s) if s < 4 else shift(s - 3)

    sib = at(y, cc=1 - c)
    xpart = at(y, xx=1 - xh)
    pair = at(shift(1))

    bar = pltpu.get_barrier_semaphore()

    def greet(dev):
        pl.semaphore_signal(bar, inc=1, device_id=dev, device_id_type=MESH)

    for s in range(1, 8):
        greet(at(slot_y(s)))
    greet(xpart)
    greet(sib)
    greet(at(y, pp=prv))
    greet(at(y, xx=1 - xh, pp=prv))
    for off in OFFSETS:
        greet(at(shift(off), pp=prv))

    nsem = [0]
    nlocal = [0]
    sends = []

    def ids(n):
        first = nsem[0]
        nsem[0] += n
        return first

    def local(src, dst):
        cp = pltpu.make_async_copy(src, dst, lsem.at[nlocal[0]])
        nlocal[0] += 1
        cp.start()
        return cp

    def push(src, dst, dev, s_id, r_id=None):
        cp = pltpu.make_async_remote_copy(
            src_ref=src, dst_ref=dst, send_sem=ssem.at[s_id],
            recv_sem=rsem.at[s_id if r_id is None else r_id],
            device_id=dev, device_id_type=MESH,
        )
        cp.start()
        sends.append(cp)

    def got(dst, r_id):
        pltpu.make_async_remote_copy(
            src_ref=dst, dst_ref=dst, send_sem=ssem.at[0], recv_sem=rsem.at[r_id],
            device_id=sib, device_id_type=MESH,
        ).wait_recv()

    l_xb = local(xb_hbm, xb)
    l_g = local(g_hbm, g)
    l_xf = local(xf_hbm, xf)
    l_up = local(up_hbm, up.at[:, pl.ds(0, HID)])
    l_dn = local(dn_hbm, dn.at[pl.ds(0, HID)])
    my_w = y * 2 + xh
    l_w = local(w_hbm, wg.at[0, my_w, c])

    mask_b = chosen_mask(rb_ref)
    mask_f = chosen_mask(rf_ref)
    sel_b = slot_select(mask_b)
    sel_f = slot_select(mask_f)
    pick_b = sel_b.T[:SLOTS].astype(BF16)
    pick_f = sel_f.T[:SLOTS].astype(BF16)

    l_xb.wait()
    l_g.wait()
    for i in range(7):
        cols = pl.ds(i * 512, 512)
        a = dot(pick_b, xb[:, cols]).reshape(FLIGHT, CAP, 512)
        b = dot(pick_b, g[:, cols]).reshape(FLIGHT, CAP, 512)
        pb[:, :, cols] = jnp.concatenate([a, b], axis=1).astype(BF16)

    pl.semaphore_wait(bar, 14)

    def up_part(k, rows):
        return up.at[rows, pl.ds(k * HID, HID)]

    def dn_part(k, rows):
        return dn.at[pl.ds(k * HID + rows.start, rows.size)]

    up_rows = [pl.ds(i * HALF, HALF) for i in range(2)]
    dn_rows = [pl.ds(i * (HID // DN), HID // DN) for i in range(DN)]
    ux, us, uy, dx, ds_, dy = ids(2), ids(2), ids(2), ids(DN), ids(DN), ids(DN)

    def enter(src, rows, iy):
        push(src.at[e], rows.at[4], pair, iy + 4)
        for off in OFFSETS:
            t = shift(off)
            push(src.at[t // 2], rows.at[abs(off)], at(t), iy + abs(off))
        return local(src.at[e], rows.at[0])

    def hands(rows, iy, slots):
        for s in slots:
            got(rows.at[s], iy + s)
            push(rows.at[s], rows.at[4 + s], pair, iy + 4 + s)

    iy_b, iy_f = ids(8), ids(8)
    l_b0 = enter(pb, rows_b, iy_b)
    for i in range(2):
        push(up_hbm.at[up_rows[i]], up_part(1, up_rows[i]), sib, us + i)
    for i in range(DN):
        push(dn_hbm.at[dn_rows[i]], dn_part(1, dn_rows[i]), sib, ds_ + i)
    wx = ids(3)
    push(w_hbm, wg.at[0, my_w, c], xpart, wx)
    push(w_hbm, wg.at[1, my_w, c], at(y, pp=nxt), wx + 1)
    push(w_hbm, wg.at[1, my_w, c], at(y, xx=1 - xh, pp=nxt), wx + 2)

    l_xf.wait()
    for i in range(7):
        lo = pl.ds(i * 256, 256)
        hi = pl.ds(HALF + i * 256, 256)
        a = dot(pick_f, xf[:, lo]).reshape(FLIGHT, CAP, 256)
        b = dot(pick_f, xf[:, hi]).reshape(FLIGHT, CAP, 256)
        pf[:, :, lo] = jnp.concatenate([a, b], axis=1).astype(BF16)

    l_f0 = enter(pf, rows_f, iy_f)

    up_dev, down_dev = at((y + 1) % NY), at((y + NY - 1) % NY)
    wr = ids(16)

    def ring(step):
        yu = (y + NY - step) % NY
        yd = (y + step) % NY
        for xx in range(2):
            if step < 3 or xx == 0:
                push(wg.at[:, yu * 2 + xx, c], wg.at[:, yu * 2 + xx, c], up_dev, wr + step * 2 + xx)
            if step < 3 or xx == 1:
                push(wg.at[:, yd * 2 + xx, c], wg.at[:, yd * 2 + xx, c], down_dev, wr + 8 + step * 2 + xx)

    wsib = ids(18)

    def to_sibling(idx, n):
        push(wg.at[:, idx, c], wg.at[:, idx, c], sib, wsib + n)

    def from_sibling(idx, n):
        got(wg.at[:, idx, 1 - c], wsib + n)

    def ring_blocks(step):
        yu = (y + NY - step - 1) % NY
        yd = (y + step + 1) % NY
        for xx in range(2):
            if step < 3 or xx == 0:
                yield yu * 2 + xx, step * 2 + xx
            if step < 3 or xx == 1:
                yield yd * 2 + xx, 8 + step * 2 + xx

    def ring_got(step):
        for idx, n in ring_blocks(step):
            got(wg.at[:, idx, c], wr + n)
            to_sibling(idx, n)

    own, other = pl.ds(0, 2 * HID), pl.ds(2 * HID, 2 * HID)

    def forward_pre(lanes):
        r = rows_f[...].reshape(128, HALF)
        low = dot(r, up[pl.ds(0, HALF), lanes]).reshape(8, 16, 256)[:, :CAP]
        high = dot(r, up[pl.ds(HALF, HALF), lanes]).reshape(8, 16, 256)[:, CAP:]
        pre_f[:, lanes] = (low + high).reshape(64, 256)

    def backward_pre(lanes):
        r = rows_b[...].reshape(128, D)
        pre_b[:, lanes] = dot(r, up[:, lanes]).reshape(8, 16, 256)[:, :CAP].reshape(64, 256)

    def backward_grad(lanes):
        r = rows_b[...].reshape(128, D)
        grad_b[:, lanes] = across(r, dn[lanes, :]).reshape(8, 16, 256)[:, CAP:].reshape(64, 256)


    def up_on(i):
        got(up_part(2, up_rows[i]), ux + i)
        push(up_part(2, up_rows[i]), up_part(3, up_rows[i]), sib, uy + i)

    def dn_on(i):
        got(dn_part(2, dn_rows[i]), dx + i)
        push(dn_part(2, dn_rows[i]), dn_part(3, dn_rows[i]), sib, dy + i)

    def send_up(i):
        push(up_hbm.at[up_rows[i]], up_part(2, up_rows[i]), xpart, ux + i)

    def send_dn(i):
        push(dn_hbm.at[dn_rows[i]], dn_part(2, dn_rows[i]), xpart, dx + i)

    send_up(0)
    send_up(1)
    for i in range(DN):
        send_dn(i)
    hands(rows_b, iy_b, (1,))
    l_w.wait()
    their_w = y * 2 + (1 - xh)
    got(wg.at[0, their_w, c], wx)
    got(wg.at[1, my_w, c], wx + 1)
    got(wg.at[1, their_w, c], wx + 2)
    ring(0)
    to_sibling(my_w, 16)
    to_sibling(their_w, 17)
    hands(rows_b, iy_b, (2, 3))
    hands(rows_f, iy_f, (1, 2, 3))
    ring_got(0)
    ring(1)
    l_b0.wait()
    l_f0.wait()
    l_up.wait()
    l_dn.wait()
    for i in range(2):
        got(up_part(1, up_rows[i]), us + i)
    for i in range(DN):
        got(dn_part(1, dn_rows[i]), ds_ + i)
    for s in range(4, 8):
        got(rows_b.at[s], iy_b + s)
    backward_pre(own)
    backward_grad(own)
    ring_got(1)
    ring(2)
    up_on(0)
    for s in range(4, 8):
        got(rows_f.at[s], iy_f + s)
    forward_pre(own)
    ring_got(2)
    ring(3)
    up_on(1)
    for i in range(2):
        got(up_part(3, up_rows[i]), uy + i)
    backward_pre(other)
    forward_pre(other)
    ring_got(3)
    for i in range(DN):
        dn_on(i)
    for i in range(DN):
        got(dn_part(3, dn_rows[i]), dy + i)
    backward_grad(other)
    pre = pre_b[...]
    act_grad = grad_b[...]
    s = sigmoid(pre)
    act = (pre * s).astype(BF16).astype(F32)
    dots = jnp.sum(act * act_grad, axis=1, keepdims=True)
    send_dot[...] = jnp.broadcast_to(dots, (64, 128)).reshape(8, CAP, 128)
    pre_grad = (act_grad * (s * (1.0 + pre * (1.0 - s)))).astype(BF16)
    back_b, back_f = ids(2), ids(2)
    for i in range(2):
        a = across(pre_grad, up[pl.ds(i * PART, PART), :]).reshape(8, CAP, PART)
        b = across(pre_grad, up[pl.ds(HALF + i * PART, PART), :]).reshape(8, CAP, PART)
        out_b[i] = jnp.concatenate([a, b], axis=1).astype(BF16)
        push(out_b.at[i, pl.ds(4, 4)], pr_b.at[i], pair, back_b + i)
    mine = e * 2 + y % 2
    dt_s, dt_r = ids(8), ids(8)
    for k in range(1, 8):
        push(send_dot.at[k], got_dot.at[mine], at(slot_y(k)), dt_s + k, dt_r + mine)
    l_dot = local(send_dot.at[0], got_dot.at[mine])

    pre = pre_f[...]
    act_f = (pre * sigmoid(pre)).astype(BF16)
    for i in range(2):
        a = dot(act_f, dn[:, pl.ds(i * PART, PART)]).reshape(8, CAP, PART)
        b = dot(act_f, dn[:, pl.ds(HALF + i * PART, PART)]).reshape(8, CAP, PART)
        out_f[i] = jnp.concatenate([a, b], axis=1).astype(BF16)
        push(out_f.at[i, pl.ds(4, 4)], pr_f.at[i], pair, back_f + i)

    hs_b, hr_b, hs_f, hr_f = ids(8), ids(8), ids(8), ids(8)

    def finish(i, out, pr, fs, fin, arrived, s_id, r_id):
        got(pr.at[i], arrived + i)
        for k in (3, 2, 1, 0):
            fs[i, k] = (out[i, k].astype(F32) + pr[i, k].astype(F32)).astype(BF16)
            push(fs.at[i, k], fin.at[i, e], at(shift(-k), pp=nxt), s_id + i * 4 + k, r_id + i * 4 + e)

    for i in range(2):
        finish(i, out_b, pr_b, fs_b, fin_b, back_b, hs_b, hr_b)

    from_sibling(my_w, 16)
    from_sibling(their_w, 17)
    for step in range(4):
        for idx, n in ring_blocks(step):
            from_sibling(idx, n)

    def scores(x):
        total = jnp.zeros((TOK, EXPERTS), F32)
        for i in range(4):
            w = wg[0, pl.ds(4 * i, 4)].reshape(896, EXPERTS)
            total = total + dot(x[:, pl.ds(896 * i, 896)], w)
        return sigmoid(total)

    score_f = scores(xf)
    score_b = scores(xb)
    sum_f = jnp.sum(mask_f * score_f, axis=1, keepdims=True)
    sum_b = jnp.sum(mask_b * score_b, axis=1, keepdims=True)
    gate_f = sel_f * to_slots(ROUTE_SCALE * score_f / sum_f)
    gate_b = sel_b * to_slots(ROUTE_SCALE * score_b / sum_b)
    msg[0], msg[1] = two_parts(gate_f)
    msg[2], msg[3] = two_parts(gate_b)
    mg = ids(1)
    push(msg, msg_in, at(y, pp=nxt), mg)

    l_dot.wait()
    for k in range(1, 8):
        source = (mine + k) % 8
        got(got_dot.at[source], dt_r + source)
    all_dots = got_dot[...].reshape(FLIGHT, 2, CAP, 128)
    slot_dots = (all_dots[:, 0] + all_dots[:, 1]).reshape(SLOTS, 128)
    slot_row = lax.broadcasted_iota(jnp.int32, (SLOTS, EXPERTS), 0)
    slot_col = lax.broadcasted_iota(jnp.int32, (SLOTS, EXPERTS), 1)
    by_expert = jnp.where(
        slot_row // CAP == slot_col, jnp.broadcast_to(slot_dots[:, 0:1], (SLOTS, EXPERTS)), 0.0
    )
    gate_grad = exact(sel_b[:, :SLOTS], by_expert)
    weighted = jnp.sum(gate_grad * score_b, axis=1, keepdims=True) / sum_b
    pick_grad = ROUTE_SCALE / sum_b * (gate_grad - weighted)
    logit_grad = (mask_b * pick_grad * score_b * (1.0 - score_b)).astype(BF16)
    lg[...] = logit_grad
    lid = ids(1)
    push(lg, lg_in, at(y, pp=nxt), lid)

    for i in range(2):
        finish(i, out_f, pr_f, fs_f, fin_f, back_f, hs_f, hr_f)

    def halves(fin, i):
        t = fin[i].astype(F32)
        return t[:, :CAP].reshape(SLOTS, PART).astype(BF16), t[:, CAP:].reshape(SLOTS, PART).astype(BF16)

    def arrived(fin, i, r_id):
        for k in range(4):
            source = (e + k) % 4
            got(fin.at[i, source], r_id + i * 4 + source)

    def router(i):
        return across(lg_in[...], wg[1, pl.ds(4 * i, 4)].reshape(PART, EXPERTS))

    got(msg_in, mg)
    got(lg_in, lid)
    f_high, f_low = msg_in[0][:, :SLOTS], msg_in[1][:, :SLOTS]
    b_high, b_low = msg_in[2][:, :SLOTS], msg_in[3][:, :SLOTS]
    for i in range(2):
        arrived(fin_b, i, hr_b)
        a, b = halves(fin_b, i)
        ob_ref[:, pl.ds(i * PART, PART)] = (dot(b_high, a) + dot(b_low, a) + router(i)).astype(BF16)
        ob_ref[:, pl.ds(HALF + i * PART, PART)] = (dot(b_high, b) + dot(b_low, b) + router(2 + i)).astype(BF16)
    for i in range(2):
        arrived(fin_f, i, hr_f)
        a, b = halves(fin_f, i)
        of_ref[:, pl.ds(i * PART, PART)] = (dot(f_high, a) + dot(f_low, a)).astype(BF16)
        of_ref[:, pl.ds(HALF + i * PART, PART)] = (dot(f_high, b) + dot(f_low, b)).astype(BF16)

    for cp in sends:
        cp.wait_send()


N_SEM = 192


def on_device(xf, xb, g, rf, rb, w, up, dn):
    vm = pltpu.VMEM
    scratch = [
        vm((TOK, D), BF16), vm((TOK, D), BF16), vm((TOK, D), BF16),
        vm((D, 4 * HID), BF16), vm((4 * HID, D), BF16), vm((2, 16, 2, WROWS, EXPERTS), BF16),
        vm((FLIGHT, 16, D), BF16), vm((FLIGHT, 16, HALF), BF16),
        vm((8, 16, D), BF16), vm((8, 16, HALF), BF16),
        vm((64, 4 * HID), F32), vm((64, 4 * HID), F32), vm((64, 4 * HID), F32),
        vm((8, CAP, 128), F32), vm((8, CAP, 128), F32),
        vm((2, 8, 16, PART), BF16), vm((2, 8, 16, PART), BF16),
        vm((2, 4, 16, PART), BF16), vm((2, 4, 16, PART), BF16),
        vm((2, 4, 16, PART), BF16), vm((2, 4, 16, PART), BF16),
        vm((2, 4, 16, PART), BF16), vm((2, 4, 16, PART), BF16),
        vm((4, TOK, 128), BF16), vm((4, TOK, 128), BF16),
        vm((TOK, EXPERTS), BF16), vm((TOK, EXPERTS), BF16),
        pltpu.SemaphoreType.DMA((16,)),
        pltpu.SemaphoreType.DMA((N_SEM,)),
        pltpu.SemaphoreType.DMA((N_SEM,)),
    ]
    hbm = pl.BlockSpec(memory_space=pl.ANY)
    vmem = pl.BlockSpec(memory_space=pltpu.VMEM)
    of, ob = pl.pallas_call(
        kernel,
        out_shape=[jax.ShapeDtypeStruct((TOK, D), BF16)] * 2,
        in_specs=[hbm, hbm, hbm, vmem, vmem, hbm, hbm, hbm],
        out_specs=[vmem, vmem],
        scratch_shapes=scratch,
        compiler_params=pltpu.CompilerParams(
            collective_id=0, has_side_effects=True, vmem_limit_bytes=60 * 2**20
        ),
        cost_estimate=pl.CostEstimate(flops=2 * 10**9, bytes_accessed=6 * 10**6, transcendentals=10**5),
        name="expert_layer",
    )(xf[0], xb[0], g[0], rf[0].T, rb[0].T, w[0], up[0], dn[0])
    return of[None], ob[None]


def solution(mesh):
    rows = P("pipe", "expert", None)
    return jax.shard_map(
        on_device,
        mesh=mesh,
        in_specs=(rows, rows, rows, rows, rows, rows, P("pipe", None, "expert"), rows),
        out_specs=(rows, rows),
        check_vma=False,
    )
```

time: 110 us -> 92.9 us (0.84); the launches traced: 109 us -> 92.7 us
  Pallas kernels: 103 us -> 89.5 us
  local copies, waits for them, and re-layouts: 4.72 us -> 2.64 us
    pallas_call x1, Pallas kernels: 103 us -> 89.5 us  [on_device(): pl.pallas_call(kernel, out_shape=[jax.ShapeDtypeStruct((TOK, D), BF16)] *...]
    unnamed x10 -> x4, local copies, waits for them, and re-layouts: 4.72 us -> 2.64 us
where the time goes in v2:
time: 92.9 us; the launch traced here: 92.7 us
  Pallas kernels  89.5 us (96%)
  local copies, waits for them, and re-layouts  2.64 us (3%)
    pallas_call x1, Pallas kernels, on_device(): pl.pallas_call(kernel, out_shape=[jax.ShapeDtypeStruct((TOK, D), BF16)] *...  89.5 us
    unnamed x4, local copies, waits for them, and re-layouts  2.64 us

profile of v2, /device:TPU:1, one launch (start us, length us, event | category | flops | bytes accessed | tf_op | source)
XLA Modules:
  0.0 92.7 jit_solution(14112626160953997057)
XLA Ops:
  0.6 89.5 %expert_layer.1 = (bf16[64,3584]{1,0:T(8,128)(2,1)}, bf16[64,3584]{1,0:T(8,128)(2,1)}) custom-call(bf16[64,3584]{1,0:T(8,128)(2,1)} %bitcast.18, bf16[64,3584]{1,0:T(8,128)(2,1)} %bitcast.19, bf16[64,3584]{1,0:T(8,128)(2,1)} %bitcast.20, s32[8,64]{1,0:T(8,128)} %bitcast.22, s32[8,64]{1,0:T(8,128)} %bitcast.23, bf16[112,256]{1,0:T(8,128)(2,1)} %bitcast.21, ...), custom_call_target="tpu_custom_call" | custom-call | flops 2000000000 | bytes 6000000 | tf_op jit(solution)/shard_map/expert_layer/pallas_call | solution.py:480
  90.1 0.0 copy-start
  90.1 1.9 %copy.12 = bf16[1,64,3584]{2,1,0:T(8,128)(2,1)} copy(bf16[1,64,3584]{2,1,0:T(8,128)(2,1)} %bitcast.15) | data formatting | bytes 917504
  92.0 0.0 copy-done
  92.0 0.8 copy.13
Async XLA Ops:
  90.1 1.9 %copy-start = (bf16[64,3584]{1,0:T(8,128)(2,1)S(1)}, bf16[64,3584]{1,0:T(8,128)(2,1)}, u32[]{:S(2)}) copy-start(bf16[64,3584]{1,0:T(8,128)(2,1)} %get-tuple-element.5) | copy-start | bytes 1376260

commit v3 on v2

--- a/solution.py
+++ b/solution.py
@@ -337,6 +337,15 @@
         dn_on(i)
     for i in range(DN):
         got(dn_part(3, dn_rows[i]), dy + i)
+    back_b, back_f = ids(2), ids(2)
+    pre = pre_f[...]
+    act_f = (pre * sigmoid(pre)).astype(BF16)
+    for i in range(2):
+        a = dot(act_f, dn[:, pl.ds(i * PART, PART)]).reshape(8, CAP, PART)
+        b = dot(act_f, dn[:, pl.ds(HALF + i * PART, PART)]).reshape(8, CAP, PART)
+        out_f[i] = jnp.concatenate([a, b], axis=1).astype(BF16)
+        push(out_f.at[i, pl.ds(4, 4)], pr_f.at[i], pair, back_f + i)
+
     backward_grad(other)
     pre = pre_b[...]
     act_grad = grad_b[...]
@@ -345,7 +354,6 @@
     dots = jnp.sum(act * act_grad, axis=1, keepdims=True)
     send_dot[...] = jnp.broadcast_to(dots, (64, 128)).reshape(8, CAP, 128)
     pre_grad = (act_grad * (s * (1.0 + pre * (1.0 - s)))).astype(BF16)
-    back_b, back_f = ids(2), ids(2)
     for i in range(2):
         a = across(pre_grad, up[pl.ds(i * PART, PART), :]).reshape(8, CAP, PART)
         b = across(pre_grad, up[pl.ds(HALF + i * PART, PART), :]).reshape(8, CAP, PART)
@@ -357,14 +365,6 @@
         push(send_dot.at[k], got_dot.at[mine], at(slot_y(k)), dt_s + k, dt_r + mine)
     l_dot = local(send_dot.at[0], got_dot.at[mine])
 
-    pre = pre_f[...]
-    act_f = (pre * sigmoid(pre)).astype(BF16)
-    for i in range(2):
-        a = dot(act_f, dn[:, pl.ds(i * PART, PART)]).reshape(8, CAP, PART)
-        b = dot(act_f, dn[:, pl.ds(HALF + i * PART, PART)]).reshape(8, CAP, PART)
-        out_f[i] = jnp.concatenate([a, b], axis=1).astype(BF16)
-        push(out_f.at[i, pl.ds(4, 4)], pr_f.at[i], pair, back_f + i)
-
     hs_b, hr_b, hs_f, hr_f = ids(8), ids(8), ids(8), ids(8)
 
     def finish(i, out, pr, fs, fin, arrived, s_id, r_id):
@@ -374,7 +374,7 @@
             push(fs.at[i, k], fin.at[i, e], at(shift(-k), pp=nxt), s_id + i * 4 + k, r_id + i * 4 + e)
 
     for i in range(2):
-        finish(i, out_b, pr_b, fs_b, fin_b, back_b, hs_b, hr_b)
+        finish(i, out_f, pr_f, fs_f, fin_f, back_f, hs_f, hr_f)
 
     from_sibling(my_w, 16)
     from_sibling(their_w, 17)
@@ -399,6 +399,9 @@
     msg[2], msg[3] = two_parts(gate_b)
     mg = ids(1)
     push(msg, msg_in, at(y, pp=nxt), mg)
+
+    for i in range(2):
+        finish(i, out_b, pr_b, fs_b, fin_b, back_b, hs_b, hr_b)
 
     l_dot.wait()
     for k in range(1, 8):
@@ -419,9 +422,6 @@
     lid = ids(1)
     push(lg, lg_in, at(y, pp=nxt), lid)
 
-    for i in range(2):
-        finish(i, out_f, pr_f, fs_f, fin_f, back_f, hs_f, hr_f)
-
     def halves(fin, i):
         t = fin[i].astype(F32)
         return t[:, :CAP].reshape(SLOTS, PART).astype(BF16), t[:, CAP:].reshape(SLOTS, PART).astype(BF16)
@@ -435,19 +435,19 @@
         return across(lg_in[...], wg[1, pl.ds(4 * i, 4)].reshape(PART, EXPERTS))
 
     got(msg_in, mg)
-    got(lg_in, lid)
     f_high, f_low = msg_in[0][:, :SLOTS], msg_in[1][:, :SLOTS]
     b_high, b_low = msg_in[2][:, :SLOTS], msg_in[3][:, :SLOTS]
+    for i in range(2):
+        arrived(fin_f, i, hr_f)
+        a, b = halves(fin_f, i)
+        of_ref[:, pl.ds(i * PART, PART)] = (dot(f_high, a) + dot(f_low, a)).astype(BF16)
+        of_ref[:, pl.ds(HALF + i * PART, PART)] = (dot(f_high, b) + dot(f_low, b)).astype(BF16)
+    got(lg_in, lid)
     for i in range(2):
         arrived(fin_b, i, hr_b)
         a, b = halves(fin_b, i)
         ob_ref[:, pl.ds(i * PART, PART)] = (dot(b_high, a) + dot(b_low, a) + router(i)).astype(BF16)
         ob_ref[:, pl.ds(HALF + i * PART, PART)] = (dot(b_high, b) + dot(b_low, b) + router(2 + i)).astype(BF16)
-    for i in range(2):
-        arrived(fin_f, i, hr_f)
-        a, b = halves(fin_f, i)
-        of_ref[:, pl.ds(i * PART, PART)] = (dot(f_high, a) + dot(f_low, a)).astype(BF16)
-        of_ref[:, pl.ds(HALF + i * PART, PART)] = (dot(f_high, b) + dot(f_low, b)).astype(BF16)
 
     for cp in sends:
         cp.wait_send()
@@ -479,7 +479,7 @@
     vmem = pl.BlockSpec(memory_space=pltpu.VMEM)
     of, ob = pl.pallas_call(
         kernel,
-        out_shape=[jax.ShapeDtypeStruct((TOK, D), BF16)] * 2,
+        out_shape=[pltpu.VMEM((TOK, D), BF16)] * 2,
         in_specs=[hbm, hbm, hbm, vmem, vmem, hbm, hbm, hbm],
         out_specs=[vmem, vmem],
         scratch_shapes=scratch,

time: 92.9 us -> 90.3 us (0.972)
  Pallas kernels: 89.5 us -> 87.9 us
  local copies, waits for them, and re-layouts: 2.64 us -> 1.54 us
    pallas_call x1, Pallas kernels: 89.5 us -> 87.9 us  [on_device(): pl.pallas_call(kernel, out_shape=[pltpu.VMEM((TOK, D), BF16)] * 2, in_spe...]
    unnamed x4 -> x2, local copies, waits for them, and re-layouts: 2.64 us -> 1.54 us
where the time goes in v3:
time: 90.3 us; the launch traced here: 90.1 us
  Pallas kernels  87.9 us (97%)
  local copies, waits for them, and re-layouts  1.54 us (2%)
    pallas_call x1, Pallas kernels, on_device(): pl.pallas_call(kernel, out_shape=[pltpu.VMEM((TOK, D), BF16)] * 2, in_spe...  87.9 us

profile of v3, /device:TPU:1, one launch (start us, length us, event | category | flops | bytes accessed | tf_op | source)
XLA Modules:
  0.0 90.1 jit_solution(1266465859820522439)
XLA Ops:
  0.6 87.9 %expert_layer.1 = (bf16[64,3584]{1,0:T(8,128)(2,1)S(1)}, bf16[64,3584]{1,0:T(8,128)(2,1)S(1)}) custom-call(bf16[64,3584]{1,0:T(8,128)(2,1)} %bitcast.18, bf16[64,3584]{1,0:T(8,128)(2,1)} %bitcast.19, bf16[64,3584]{1,0:T(8,128)(2,1)} %bitcast.20, s32[8,64]{1,0:T(8,128)} %bitcast.22, s32[8,64]{1,0:T(8,128)} %bitcast.23, bf16[112,256]{1,0:T(8,128)(2,1)} %bitcast.21, ...), custom_call_target="tpu_custom_call" | custom-call | flops 2000000000 | bytes 6000000 | tf_op jit(solution)/shard_map/expert_layer/pallas_call | solution.py:480
  88.6 0.8 copy.12
  89.3 0.8 copy.13

commit v4 on v3

--- a/solution.py
+++ b/solution.py
@@ -185,11 +185,11 @@
     def up_part(k, rows):
         return up.at[rows, pl.ds(k * HID, HID)]
 
-    def dn_part(k, rows):
-        return dn.at[pl.ds(k * HID + rows.start, rows.size)]
+    def dn_part(k, cols):
+        return dn.at[pl.ds(k * HID, HID), cols]
 
     up_rows = [pl.ds(i * HALF, HALF) for i in range(2)]
-    dn_rows = [pl.ds(i * (HID // DN), HID // DN) for i in range(DN)]
+    dn_cols = [pl.ds(i * PART, PART) for i in (0, 2, 1, 3)]
     ux, us, uy, dx, ds_, dy = ids(2), ids(2), ids(2), ids(DN), ids(DN), ids(DN)
 
     def enter(src, rows, iy):
@@ -209,7 +209,7 @@
     for i in range(2):
         push(up_hbm.at[up_rows[i]], up_part(1, up_rows[i]), sib, us + i)
     for i in range(DN):
-        push(dn_hbm.at[dn_rows[i]], dn_part(1, dn_rows[i]), sib, ds_ + i)
+        push(dn_hbm.at[:, dn_cols[i]], dn_part(1, dn_cols[i]), sib, ds_ + i)
     wx = ids(3)
     push(w_hbm, wg.at[0, my_w, c], xpart, wx)
     push(w_hbm, wg.at[1, my_w, c], at(y, pp=nxt), wx + 1)
@@ -281,14 +281,14 @@
         push(up_part(2, up_rows[i]), up_part(3, up_rows[i]), sib, uy + i)
 
     def dn_on(i):
-        got(dn_part(2, dn_rows[i]), dx + i)
-        push(dn_part(2, dn_rows[i]), dn_part(3, dn_rows[i]), sib, dy + i)
+        got(dn_part(2, dn_cols[i]), dx + i)
+        push(dn_part(2, dn_cols[i]), dn_part(3, dn_cols[i]), sib, dy + i)
 
     def send_up(i):
         push(up_hbm.at[up_rows[i]], up_part(2, up_rows[i]), xpart, ux + i)
 
     def send_dn(i):
-        push(dn_hbm.at[dn_rows[i]], dn_part(2, dn_rows[i]), xpart, dx + i)
+        push(dn_hbm.at[:, dn_cols[i]], dn_part(2, dn_cols[i]), xpart, dx + i)
 
     send_up(0)
     send_up(1)
@@ -314,7 +314,7 @@
     for i in range(2):
         got(up_part(1, up_rows[i]), us + i)
     for i in range(DN):
-        got(dn_part(1, dn_rows[i]), ds_ + i)
+        got(dn_part(1, dn_cols[i]), ds_ + i)
     for s in range(4, 8):
         got(rows_b.at[s], iy_b + s)
     backward_pre(own)
@@ -332,20 +332,23 @@
         got(up_part(3, up_rows[i]), uy + i)
     backward_pre(other)
     forward_pre(other)
-    ring_got(3)
-    for i in range(DN):
-        dn_on(i)
-    for i in range(DN):
-        got(dn_part(3, dn_rows[i]), dy + i)
     back_b, back_f = ids(2), ids(2)
     pre = pre_f[...]
     act_f = (pre * sigmoid(pre)).astype(BF16)
-    for i in range(2):
+
+    def forward_out(i):
+        for j in (2 * i, 2 * i + 1):
+            dn_on(j)
+        for j in (2 * i, 2 * i + 1):
+            got(dn_part(3, dn_cols[j]), dy + j)
         a = dot(act_f, dn[:, pl.ds(i * PART, PART)]).reshape(8, CAP, PART)
         b = dot(act_f, dn[:, pl.ds(HALF + i * PART, PART)]).reshape(8, CAP, PART)
         out_f[i] = jnp.concatenate([a, b], axis=1).astype(BF16)
         push(out_f.at[i, pl.ds(4, 4)], pr_f.at[i], pair, back_f + i)
 
+    forward_out(0)
+    ring_got(3)
+    forward_out(1)
     backward_grad(other)
     pre = pre_b[...]
     act_grad = grad_b[...]

time: 90.3 us -> 87.7 us (0.971)
  Pallas kernels: 87.9 us -> 85.4 us
    pallas_call x1, Pallas kernels: 87.9 us -> 85.4 us  [on_device(): pl.pallas_call(kernel, out_shape=[pltpu.VMEM((TOK, D), BF16)] * 2, in_spe...]
where the time goes in v4:
time: 87.7 us; the launch traced here: 87.5 us
  Pallas kernels  85.4 us (97%)
  local copies, waits for them, and re-layouts  1.54 us (2%)
    pallas_call x1, Pallas kernels, on_device(): pl.pallas_call(kernel, out_shape=[pltpu.VMEM((TOK, D), BF16)] * 2, in_spe...  85.4 us

profile of v4, /device:TPU:1, one launch (start us, length us, event | category | flops | bytes accessed | tf_op | source)
XLA Modules:
  0.0 87.5 jit_solution(12610414480327210571)
XLA Ops:
  0.6 85.4 %expert_layer.1 = (bf16[64,3584]{1,0:T(8,128)(2,1)S(1)}, bf16[64,3584]{1,0:T(8,128)(2,1)S(1)}) custom-call(bf16[64,3584]{1,0:T(8,128)(2,1)} %bitcast.18, bf16[64,3584]{1,0:T(8,128)(2,1)} %bitcast.19, bf16[64,3584]{1,0:T(8,128)(2,1)} %bitcast.20, s32[8,64]{1,0:T(8,128)} %bitcast.22, s32[8,64]{1,0:T(8,128)} %bitcast.23, bf16[112,256]{1,0:T(8,128)(2,1)} %bitcast.21, ...), custom_call_target="tpu_custom_call" | custom-call | flops 2000000000 | bytes 6000000 | tf_op jit(solution)/shard_map/expert_layer/pallas_call | solution.py:483
  86.0 0.8 copy.12
  86.8 0.8 copy.13

commit v5 on v4

--- a/solution.py
+++ b/solution.py
@@ -345,11 +345,15 @@
         b = dot(act_f, dn[:, pl.ds(HALF + i * PART, PART)]).reshape(8, CAP, PART)
         out_f[i] = jnp.concatenate([a, b], axis=1).astype(BF16)
         push(out_f.at[i, pl.ds(4, 4)], pr_f.at[i], pair, back_f + i)
+        share = jnp.zeros((128, 2 * HID), F32)
+        for j in (2 * i, 2 * i + 1):
+            share = share + across(rows_b[:, :, dn_cols[j]].reshape(128, PART), dn[other, dn_cols[j]])
+        share = share.reshape(8, 16, 2 * HID)[:, CAP:].reshape(64, 2 * HID)
+        grad_b[:, other] = share if i == 0 else grad_b[:, other] + share
 
     forward_out(0)
     ring_got(3)
     forward_out(1)
-    backward_grad(other)
     pre = pre_b[...]
     act_grad = grad_b[...]
     s = sigmoid(pre)

time: 87.7 us -> 87.5 us (level)
  no operation moved by 1% of the time
where the time goes in v5:
time: 87.5 us; the launch traced here: 87.4 us
  Pallas kernels  85.2 us (97%)
  local copies, waits for them, and re-layouts  1.54 us (2%)
    pallas_call x1, Pallas kernels, on_device(): pl.pallas_call(kernel, out_shape=[pltpu.VMEM((TOK, D), BF16)] * 2, in_spe...  85.2 us

profile of v5, /device:TPU:1, one launch (start us, length us, event | category | flops | bytes accessed | tf_op | source)
XLA Modules:
  0.0 87.4 jit_solution(11156984037044580385)
XLA Ops:
  0.6 85.2 %expert_layer.1 = (bf16[64,3584]{1,0:T(8,128)(2,1)S(1)}, bf16[64,3584]{1,0:T(8,128)(2,1)S(1)}) custom-call(bf16[64,3584]{1,0:T(8,128)(2,1)} %bitcast.18, bf16[64,3584]{1,0:T(8,128)(2,1)} %bitcast.19, bf16[64,3584]{1,0:T(8,128)(2,1)} %bitcast.20, s32[8,64]{1,0:T(8,128)} %bitcast.22, s32[8,64]{1,0:T(8,128)} %bitcast.23, bf16[112,256]{1,0:T(8,128)(2,1)} %bitcast.21, ...), custom_call_target="tpu_custom_call" | custom-call | flops 2000000000 | bytes 6000000 | tf_op jit(solution)/shard_map/expert_layer/pallas_call | solution.py:487
  85.8 0.8 copy.12
  86.6 0.8 copy.13
